TPU v7x, 256 devices: a whole 4x4x8 slice. The times are simulated.
256 devices in a mesh: replica: 64 (over x, y_hi, z), fsdp: 4 (over y_lo, core).
Axes of the slice: x: 4, y: 4 (y_hi: 2, y_lo: 2; y = y_hi * 2 + y_lo), z: 8, core: 2. Of those that a mesh axis runs over, the one named last changes fastest.
Arguments:
- tokens: bfloat16 [32768, 8192], P(('replica', 'fsdp')), may hold values from -6 to 6
- norm_gain: float32 [8192], replicated, may hold values from 0.25 to 1.75
- key_weight: bfloat16 [64, 8192, 512], P('replica', 'fsdp'), may hold values from -6 to 6
- key_cotangent: bfloat16 [32768, 512], P(('replica', 'fsdp')), may hold values from -6 to 6
- fragment_local: bfloat16 [64, 8192, 512], P('replica', 'fsdp'), may hold values from -16 to 16
- fragment_global: float32 [4, 2048, 512], P('fsdp', 'replica'), may hold values from -6 to 6
- outer_moment: float32 [4, 2048, 512], P('fsdp', 'replica'), may hold values from -4 to 4
Outputs:
- key_out: bfloat16 [32768, 512], P(('replica', 'fsdp'))
- input_grad: bfloat16 [32768, 8192], P(('replica', 'fsdp'))
- key_weight_new: bfloat16 [64, 8192, 512], P('replica', 'fsdp')
- fragment_mixed: bfloat16 [64, 8192, 512], P('replica', 'fsdp')
- moment_new: float32 [4, 2048, 512], P('fsdp', 'replica')
- global_new: float32 [4, 2048, 512], P('fsdp', 'replica')
All inputs are finite; a program needn't handle non-finite values.
Results may differ from a plain program's by a relative error of at most 0.014.
Values may be sent and summed in bfloat16 or wider, within the bound.
A program may use at most 128 MiB of HBM per device.

v0:
```python
import jax
import jax.numpy as jnp
from jax import lax
from jax.sharding import PartitionSpec as P

norm_eps = 1e-05
inner_rate = 1.0
outer_rate = 0.7
momentum_decay = 0.9
mix_keep = 0.5


def against_rows(left, block_rows):
    return lax.dot_general(
        left, block_rows, (((1,), (1,)), ((), ())), preferred_element_type=jnp.float32
    )


def local(
    tokens, norm_gain, key_weight, key_cotangent, fragment_local, fragment_global, outer_moment
):
    feature = tokens.astype(jnp.float32)
    model_width = feature.shape[1]
    factor = model_width ** (-0.5)
    inverse = lax.rsqrt(jnp.mean(feature * feature, axis=1, keepdims=True) + norm_eps)
    scaled = feature * inverse
    normed = (scaled * norm_gain).astype(jnp.bfloat16)
    weight_shard = key_weight[0]
    columns = normed
    key_sums = jnp.dot(
        columns,
        lax.all_gather(weight_shard, "fsdp", axis=0, tiled=True),
        preferred_element_type=jnp.float32,
    )
    back_sums = against_rows(
        key_cotangent, lax.all_gather(weight_shard, "fsdp", axis=0, tiled=True)
    )
    columns = normed
    weight_grad = lax.psum_scatter(
        (
            factor
            * lax.dot_general(
                columns, key_cotangent, (((0,), (0,)), ((), ())), preferred_element_type=jnp.float32
            )
        ).astype(jnp.bfloat16),
        "fsdp",
        scatter_dimension=0,
        tiled=True,
    ).astype(jnp.float32)
    key_out = (factor * key_sums).astype(jnp.bfloat16)
    gain_back = norm_gain * (factor * back_sums)
    input_grad = (
        inverse * (gain_back - scaled * jnp.mean(scaled * gain_back, axis=1, keepdims=True))
    ).astype(jnp.bfloat16)
    weight_new = (weight_shard.astype(jnp.float32) - inner_rate * weight_grad).astype(jnp.bfloat16)
    local_rows = fragment_local[0].astype(jnp.float32)
    share_rows = fragment_global.shape[1]
    replicas = lax.axis_size("replica")
    summed = lax.psum(local_rows, "replica")
    mean_rows = (
        lax.dynamic_slice_in_dim(summed, lax.axis_index("replica") * share_rows, share_rows, 0)
        / replicas
    )
    global_rows = fragment_global[0]
    outer_grad = global_rows - mean_rows
    moment_new = momentum_decay * outer_moment[0] + outer_grad
    global_new = global_rows - outer_rate * (outer_grad + momentum_decay * moment_new)
    gathered = lax.all_gather(global_new.astype(jnp.bfloat16), "replica", axis=0, tiled=True)
    fragment_mixed = (
        mix_keep * local_rows + (1.0 - mix_keep) * gathered.astype(jnp.float32)
    ).astype(jnp.bfloat16)
    return (
        key_out,
        input_grad,
        weight_new[None],
        fragment_mixed[None],
        moment_new[None],
        global_new[None],
    )


def solution(mesh):
    return jax.shard_map(
        local,
        mesh=mesh,
        in_specs=(
            P(("replica", "fsdp"), None),
            P(),
            P("replica", "fsdp", None),
            P(("replica", "fsdp"), None),
            P("replica", "fsdp", None),
            P("fsdp", "replica", None),
            P("fsdp", "replica", None),
        ),
        out_specs=(
            P(("replica", "fsdp"), None),
            P(("replica", "fsdp"), None),
            P("replica", "fsdp", None),
            P("replica", "fsdp", None),
            P("fsdp", "replica", None),
            P("fsdp", "replica", None),
        ),
        check_vma=False,
    )
```

profile of v0, /device:TPU:8, one launch (start us, length us, event | category | flops | bytes accessed | tf_op | source)
XLA Modules:
  0.0 1017.6 jit_solution(8862888602352091660)
XLA Ops:
  7.2 0.0 copy-start
  7.2 0.0 copy-start.3
  7.2 0.0 all-reduce.2.cloned.1.call-start
  7.3 4.2 bitcast_convert_fusion
  11.5 0.0 all-reduce.2.cloned.1.call-update
  11.5 0.0 all-gather.4.cloned.1.call-start
  11.5 708.5 %all-reduce.2.cloned.1.call-done = f32[2048,512]{1,0:T(8,128)} async-done(((f32[2048,512]{1,0:T(8,128)}), f32[2048,512]{1,0:T(8,128)}) %all-reduce.2.cloned.1.call-update) | async-done | bytes 4194320 | tf_op jit(solution)/shard_map/psum | solution.py:59
  720.1 0.0 copy-done.3
  720.1 1.5 fusion.24
  721.6 0.0 all-gather.4.cloned.1.call-update
  721.6 0.0 all-gather.6.cloned.1.call-start
  721.7 0.7 all-gather.6.cloned.1.call-update
  722.4 0.0 reduce-scatter.2.cloned.1.call-start
  722.4 0.5 fusion.11
  722.9 5.8 multiply_convert_fusion
  728.7 0.0 reduce-scatter.2.cloned.1.call-update
  728.7 111.1 %all-gather.4.cloned.1.call-done = bf16[2048,512]{1,0:T(8,128)(2,1)} async-done(((bf16[32,512]{1,0:T(8,128)(2,1)}), bf16[2048,512]{1,0:T(8,128)(2,1)}) %all-gather.4.cloned.1.call-update) | async-done | bytes 2097168 | tf_op jit(solution)/shard_map/all_gather | solution.py:68
  839.9 4.2 fusion.13
  844.1 77.6 %all-gather.6.cloned.1.call-done = bf16[1,8192,512]{2,1,0:T(8,128)(2,1)} async-done(((bf16[1,2048,512]{2,1,0:T(8,128)(2,1)}), bf16[1,8192,512]{2,1,0:T(8,128)(2,1)}) %all-gather.6.cloned.1.call-update) | async-done | bytes 8388624 | tf_op jit(solution)/shard_map/all_gather | solution.py:32
  921.7 6.5 fusion.7
  928.2 2.1 fusion.18
  930.3 2.3 fusion.10
  932.5 74.4 %reduce-scatter.2.cloned.1.call-done = bf16[2048,512]{1,0:T(8,128)(2,1)} async-done(((bf16[8192,512]{1,0:T(8,128)(2,1)}), bf16[2048,512]{1,0:T(8,128)(2,1)}) %reduce-scatter.2.cloned.1.call-update) | async-done | bytes 2097168 | tf_op jit(solution)/shard_map/reduce_scatter | solution.py:39
  1006.9 4.1 fusion.14
  (12 shorter events, 0.0 us)
Async XLA Ops:
  7.2 715.8 %copy-start = (bf16[128,512]{1,0:T(8,128)(2,1)S(1)}, bf16[128,512]{1,0:T(8,128)(2,1)}, u32[]{:S(2)}) copy-start(bf16[128,512]{1,0:T(8,128)(2,1)} %param.10) | copy-start | bytes 393220
  7.2 712.9 %copy-start.3 = (f32[1,32,512]{2,1,0:T(8,128)S(1)}, f32[1,32,512]{2,1,0:T(8,128)}, u32[]{:S(2)}) copy-start(f32[1,32,512]{2,1,0:T(8,128)} %param.13) | copy-start | bytes 196612
  7.2 712.9 %copy-start.4 = (f32[1,32,512]{2,1,0:T(8,128)S(1)}, f32[1,32,512]{2,1,0:T(8,128)}, u32[]{:S(2)}) copy-start(f32[1,32,512]{2,1,0:T(8,128)} %param.12) | copy-start | bytes 196612
  7.2 712.9 %all-reduce.2.cloned.1.call-start = ((), (), s32[]{:S(2)}) async-start(), calls=%async_computation.2 | async-start | bytes 8388608 | tf_op jit(solution)/shard_map/psum | solution.py:59
  11.5 711.0 %copy-start.1 = (bf16[128,8192]{1,0:T(8,128)(2,1)S(1)}, bf16[128,8192]{1,0:T(8,128)(2,1)}, u32[]{:S(2)}) copy-start(bf16[128,8192]{1,0:T(8,128)(2,1)} %param.7) | copy-start | bytes 6291460
  11.5 711.5 %copy-start.5 = (f32[8192]{0:T(1024)S(1)}, f32[8192]{0:T(1024)}, u32[]{:S(2)}) copy-start(f32[8192]{0:T(1024)} %param.8) | copy-start | bytes 98308
  11.5 828.4 %all-gather.4.cloned.1.call-start = ((), (), s32[]{:S(2)}) async-start(), calls=%async_computation.3 | async-start | bytes 2129920 | tf_op jit(solution)/shard_map/all_gather | solution.py:68
  721.6 200.1 %all-gather.6.cloned.1.call-start = ((), (), s32[]{:S(2)}) async-start(), calls=%async_computation.4 | async-start | bytes 10485760 | tf_op jit(solution)/shard_map/all_gather | solution.py:32
  722.4 284.6 %reduce-scatter.2.cloned.1.call-start = ((), (), s32[]{:S(2)}) async-start(), calls=%async_computation.1 | async-start | bytes 10485760 | tf_op jit(solution)/shard_map/reduce_scatter | solution.py:39
  921.7 6.5 copy-start.2
Sparse Core Ops, SparseCore 0:
  11.6 708.4 all-reduce.1
  725.0 114.8 all-gather.3
  841.8 79.8 all-gather.5
  924.4 82.5 reduce-scatter.1
where the time goes:
time: 1020 us
  waiting for transfers between devices  972 us (95%)
  other arithmetic  16.8 us (2%)
  matrix products  14.3 us (1%)
  between operations  13.8 us (1%)
    psum x1, waiting for transfers between devices, local(): summed = lax.psum(local_rows, 'replica')  709 us
    all_gather x1, waiting for transfers between devices, local(): lax.all_gather(global_new.astype(jnp.bfloat16), 'replica', axis=0, tiled=...  111 us
    all_gather x1, waiting for transfers between devices, local(): lax.all_gather(weight_shard, 'fsdp', axis=0, tiled=True)  77.6 us
    reduce_scatter x1, waiting for transfers between devices, local(): lax.psum_scatter((factor * lax.dot_general(columns, key_cotangent, (((0,)...  74.4 us
  transfers between devices with their start and end apart: 4, of which 4 were waited for; matrix products, arithmetic and copies ran while one was open for 2% of the time, Pallas kernels for 0%

commit v1 on v0

v1 whole, which is shorter than its diff:
```python
import jax
import jax.numpy as jnp
from jax import lax
from jax.experimental import pallas as pl
from jax.experimental.pallas import tpu as pltpu
from jax.sharding import PartitionSpec as P

norm_eps = 1e-05
inner_rate = 1.0
outer_rate = 0.7
momentum_decay = 0.9
mix_keep = 0.5

MESH = pl.DeviceIdType.MESH
NX, NH, NZ, NF = 4, 2, 8, 4
REPLICAS = NX * NH * NZ
TOK, D, KV = 128, 8192, 512
COLS = D // NF
SHARE = COLS // REPLICAS
XB = COLS // NX
K = 4
KC = KV // K
PARTS = 4
PR = TOK // PARTS
SLAB = 512
FACTOR = D ** (-0.5)
N_COPIES = 128
N_LOADS = 16
f32, bf16 = jnp.float32, jnp.bfloat16


def kernel(
    tokens,
    gain_in,
    weight_in,
    cot_in,
    frag_in,
    global_in,
    moment_in,
    key_out,
    input_grad,
    weight_new,
    mixed,
    moment_new,
    global_new,
    tok,
    gain,
    weight,
    frag,
    glob,
    moment,
    cot,
    nin,
    nout,
    inv_s,
    bout,
    bin_,
    kp,
    kp1,
    kx,
    ksend,
    kc,
    xr,
    s1,
    zr,
    s2,
    yr,
    gx,
    send_sem,
    recv_sem,
    load_sem,
):
    r = lax.axis_index("replica")
    f = lax.axis_index("fsdp")
    x, yh, z = r // (NH * NZ), (r // NZ) % NH, r % NZ
    yl, core = f // 2, f % 2

    def fsdp_peer(q):
        a = 1 - yl if q & 2 else yl
        b = 1 - core if q & 1 else core
        return a * 2 + b

    def x_peer(d):
        return (((x + d) % NX) * NH + yh) * NZ + z, f

    def z_peer(d):
        return (x * NH + yh) * NZ + (z + d) % NZ, f

    y_peer = ((x * NH + (1 - yh)) * NZ + z, f)
    f_peer = {q: (r, fsdp_peer(q)) for q in (1, 2, 3)}

    loads = []

    def load(src, dst):
        copy = pltpu.make_async_copy(src, dst, load_sem.at[len(loads)])
        copy.start()
        loads.append(copy)
        return copy

    def block_cols(q):
        return pl.ds(pl.multiple_of((fsdp_peer(q) if q else f) * COLS, COLS), COLS)

    load_tok = [load(tokens.at[:, block_cols(q)], tok.at[q]) for q in range(NF)]
    load_gain = [load(gain_in.at[:, block_cols(q)], gain.at[q]) for q in range(NF)]
    load_cot = load(cot_in, cot.at[0])
    load_weight = load(weight_in.at[0], weight)
    load_frag = load(frag_in.at[0], frag)
    load_outer = [load(global_in.at[0], glob), load(moment_in.at[0], moment)]

    barrier = pltpu.get_barrier_semaphore()
    peers = (
        [f_peer[q] for q in (1, 2, 3)]
        + [x_peer(d) for d in range(1, NX)]
        + [z_peer(d) for d in range(1, NZ)]
        + [y_peer]
    )
    for peer in peers:
        pl.semaphore_signal(barrier, 1, device_id=peer, device_id_type=MESH)

    copies = []

    def remote(src, dst, device):
        i = len(copies)
        copy = pltpu.make_async_remote_copy(
            src, dst, send_sem.at[i], recv_sem.at[i], device_id=device, device_id_type=MESH
        )
        copy.start()
        copies.append(copy)
        return copy

    def rows_of(c):
        return pl.ds(c * PR, PR)

    def fold(v):
        return v[:, :128] + v[:, 128:256] + v[:, 256:384] + v[:, 384:]

    def normalise(c):
        rows = rows_of(c)

        def square(q, acc):
            for s in range(COLS // SLAB):
                v = tok[q, rows, pl.ds(s * SLAB, SLAB)].astype(f32)
                acc = acc + fold(v * v)
            return acc

        acc = lax.fori_loop(0, NF, square, jnp.zeros((PR, 128), f32))
        inv = lax.rsqrt(jnp.sum(acc, axis=1, keepdims=True) * (1.0 / D) + norm_eps)
        inv_s[rows, :] = jnp.broadcast_to(inv, (PR, 128))

        def scale(q, dst):
            for s in range(COLS // SLAB):
                lanes = pl.ds(s * SLAB, SLAB)
                v = tok[q, rows, lanes].astype(f32)
                dst[q, rows, lanes] = (v * inv * gain[q, :, lanes]).astype(bf16)

        scale(0, nin)

        def others(q, _):
            scale(q, nout)
            return 0

        lax.fori_loop(1, NF, others, 0)

    def send_normed(c, q):
        return remote(nout.at[q, rows_of(c)], nin.at[q, rows_of(c)], f_peer[q])

    def back_products():
        left = cot[...].reshape(NF * TOK, KV)

        def tile(t, _):
            rows = pl.ds(pl.multiple_of(t * 256, 256), 256)
            res = lax.dot_general(
                left, weight[rows, :], (((1,), (1,)), ((), ())), preferred_element_type=f32
            )
            res = (FACTOR * res).astype(bf16)
            bin_[0, :, rows] = res[:TOK]
            for q in range(1, NF):
                bout[q, :, rows] = res[q * TOK : (q + 1) * TOK]
            return 0

        lax.fori_loop(0, COLS // 256, tile, 0)

    def send_back(c, q):
        return remote(bout.at[q, rows_of(c)], bin_.at[q, rows_of(c)], f_peer[q])

    def key_products():
        left = nin[...].reshape(NF * TOK, COLS)
        for n in range(2):
            lanes = pl.ds(n * 256, 256)
            res = jnp.dot(left, weight[:, lanes], preferred_element_type=f32)
            for q in range(NF):
                kp[q, :, lanes] = res[q * TOK : (q + 1) * TOK]

    def weight_products():
        right = cot[...].reshape(NF * TOK, KV)

        def tile(t, _):
            rows = pl.ds(pl.multiple_of(t * 256, 256), 256)
            left = nin[:, :, rows].reshape(NF * TOK, 256)
            res = lax.dot_general(
                left, right, (((0,), (0,)), ((), ())), preferred_element_type=f32
            )
            weight_new[0, rows, :] = (
                weight[rows, :].astype(f32) - inner_rate * (FACTOR * res)
            ).astype(bf16)
            return 0

        lax.fori_loop(0, COLS // 256, tile, 0)

    def finish_tokens(c):
        rows = rows_of(c)
        inv = inv_s[rows, :][:, :1]

        def project(q, acc):
            for s in range(COLS // SLAB):
                lanes = pl.ds(s * SLAB, SLAB)
                scaled = tok[q, rows, lanes].astype(f32) * inv
                gain_back = gain[q, :, lanes] * bin_[q, rows, lanes].astype(f32)
                acc = acc + fold(scaled * gain_back)
            return acc

        acc = lax.fori_loop(0, NF, project, jnp.zeros((PR, 128), f32))
        mean = jnp.sum(acc, axis=1, keepdims=True) * (1.0 / D)
        for q in range(NF):
            owner = fsdp_peer(q) if q else f
            for s in range(COLS // SLAB):
                lanes = pl.ds(s * SLAB, SLAB)
                scaled = tok[q, rows, lanes].astype(f32) * inv
                gain_back = gain[q, :, lanes] * bin_[q, rows, lanes].astype(f32)
                out = pl.ds(pl.multiple_of(owner * COLS + s * SLAB, SLAB), SLAB)
                input_grad[rows, out] = (inv * (gain_back - scaled * mean)).astype(bf16)

    def x_scatter(k):
        return [
            remote(
                frag_in.at[
                    0,
                    pl.ds(pl.multiple_of(((x + d) % NX) * XB, XB), XB),
                    pl.ds(k * KC, KC),
                ],
                xr.at[k, d - 1],
                x_peer(d),
            )
            for d in range(1, NX)
        ]

    def x_sum(k):
        lanes = pl.ds(k * KC, KC)
        for h in range(NH):
            base = ((yh + h) % NH) * (NZ * SHARE)

            def one(zi, _):
                at = base + zi * SHARE
                own = pl.ds(pl.multiple_of(x * XB + at, SHARE), SHARE)
                rows = pl.ds(pl.multiple_of(at, SHARE), SHARE)
                total = frag[own, lanes].astype(f32)
                for d in range(NX - 1):
                    total = total + xr[k, d, rows, :].astype(f32)
                s1[k, zi, h] = total
                return 0

            lax.fori_loop(0, NZ, one, 0)

    def z_scatter(k):
        return [
            remote(s1.at[k, (z + d) % NZ], zr.at[k, d - 1], z_peer(d)) for d in range(1, NZ)
        ]

    def z_sum(k):
        total = s1[k, z]
        for d in range(NZ - 1):
            total = total + zr[k, d]
        s2[k] = total

    def y_scatter(k):
        return remote(s2.at[k, 1], yr.at[k], y_peer)

    def update(k):
        lanes = pl.ds(k * KC, KC)
        mean = (s2[k, 0] + yr[k]) * (1.0 / REPLICAS)
        g = glob[:, lanes]
        outer_grad = g - mean
        m = momentum_decay * moment[:, lanes] + outer_grad
        g = g - outer_rate * (outer_grad + momentum_decay * m)
        moment_new[0, :, lanes] = m
        global_new[0, :, lanes] = g
        gx[0, k, 0, 0] = g.astype(bf16)

    def y_gather(k):
        return remote(gx.at[0, k, 0, 0], gx.at[0, k, 0, 1], y_peer)

    def z_gather(k):
        return [remote(gx.at[0, k, 0], gx.at[0, k, d], z_peer(d)) for d in range(1, NZ)]

    def x_gather(k):
        return [remote(gx.at[0, k], gx.at[e, k], x_peer(e)) for e in range(1, NX)]

    def mix(k, e):
        lanes = pl.ds(k * KC, KC)
        xi = (x + NX - e) % NX
        for h in range(NH):
            base = xi * XB + ((yh + h) % NH) * (NZ * SHARE)

            def one(d, _):
                at = base + ((z + NZ - d) % NZ) * SHARE
                rows = pl.ds(pl.multiple_of(at, SHARE), SHARE)
                mixed[0, rows, lanes] = (
                    mix_keep * frag[rows, lanes].astype(f32)
                    + (1.0 - mix_keep) * gx[e, k, d, h].astype(f32)
                ).astype(bf16)
                return 0

            lax.fori_loop(0, NZ, one, 0)

    def arrive(group):
        for copy in group if isinstance(group, list) else [group]:
            copy.wait_recv()

    for copy in load_tok + load_gain:
        copy.wait()
    normalise(0)
    pl.semaphore_wait(barrier, len(peers))
    cot1 = remote(cot_in, cot.at[1], f_peer[1])
    cot2 = remote(cot_in, cot.at[2], f_peer[2])
    xs = [x_scatter(0), x_scatter(1)]
    nq = {}
    bq = {}
    for q in (2, 3, 1):
        nq[0, q] = send_normed(0, q)
    xs += [x_scatter(2), x_scatter(3)]
    for c in range(1, PARTS):
        normalise(c)
        nq[c, 1] = send_normed(c, 1)
    arrive(cot2)
    cot3 = remote(cot.at[2], cot.at[3], f_peer[1])
    nq[1, 2] = send_normed(1, 2)

    load_frag.wait()
    arrive(xs[0])
    x_sum(0)
    zs = [z_scatter(0)]
    nq[1, 3] = send_normed(1, 3)
    nq[2, 2] = send_normed(2, 2)
    load_cot.wait()
    load_weight.wait()
    arrive(cot1)
    arrive(cot3)
    back_products()
    for c in range(PARTS):
        bq[c, 1] = send_back(c, 1)

    arrive(xs[1])
    x_sum(1)
    zs.append(z_scatter(1))
    arrive(zs[0])
    z_sum(0)
    ys = [y_scatter(0)]
    nq[2, 3] = send_normed(2, 3)
    nq[3, 2] = send_normed(3, 2)
    for copy in load_outer:
        copy.wait()

    arrive(xs[2])
    x_sum(2)
    zs.append(z_scatter(2))
    arrive(zs[1])
    z_sum(1)
    ys.append(y_scatter(1))
    arrive(ys[0])
    update(0)
    yg = [y_gather(0)]
    nq[3, 3] = send_normed(3, 3)
    bq[0, 2] = send_back(0, 2)

    arrive(xs[3])
    x_sum(3)
    zs.append(z_scatter(3))
    arrive(zs[2])
    z_sum(2)
    ys.append(y_scatter(2))
    arrive(ys[1])
    update(1)
    yg.append(y_gather(1))
    arrive(yg[0])
    zg = [z_gather(0)]
    bq[0, 3] = send_back(0, 3)
    bq[1, 2] = send_back(1, 2)

    arrive(zs[3])
    z_sum(3)
    ys.append(y_scatter(3))
    arrive(ys[2])
    update(2)
    yg.append(y_gather(2))
    arrive(yg[1])
    zg.append(z_gather(1))
    arrive(zg[0])
    xg = [x_gather(0)]
    bq[1, 3] = send_back(1, 3)
    bq[2, 2] = send_back(2, 2)
    for c in range(PARTS):
        for q in (1, 2, 3):
            arrive(nq[c, q])
    key_products()
    k3 = remote(kp.at[3], kx, f_peer[1])
    k1 = remote(kp.at[1], kp1, f_peer[1])

    arrive(ys[3])
    update(3)
    yg.append(y_gather(3))
    arrive(yg[2])
    zg.append(z_gather(2))
    arrive(zg[1])
    xg.append(x_gather(1))
    arrive(k3)
    ksend[...] = (FACTOR * (kp[2] + kx[...])).astype(bf16)
    k2 = remote(ksend, kc, f_peer[2])
    bq[2, 3] = send_back(2, 3)
    arrive(yg[3])
    zg.append(z_gather(3))
    bq[3, 2] = send_back(3, 2)
    bq[3, 3] = send_back(3, 3)
    arrive(zg[2])
    xg.append(x_gather(2))
    arrive(zg[3])
    xg.append(x_gather(3))
    weight_products()

    for k in range(K):
        mix(k, 0)
    for k in range(K):
        for c in range(PARTS):
            if c == k:
                for q in (1, 2, 3):
                    arrive(bq[c, q])
                finish_tokens(c)
        arrive(xg[k])
        for e in range(1, NX):
            mix(k, e)
        if k == 1:
            arrive(k1)
            arrive(k2)
            key_out[...] = (FACTOR * (kp[0] + kp1[...]) + kc[...].astype(f32)).astype(bf16)
    for copy in copies:
        copy.wait_send()


def local(
    tokens, norm_gain, key_weight, key_cotangent, fragment_local, fragment_global, outer_moment
):
    any_space = pl.BlockSpec(memory_space=pl.ANY)
    vmem = pl.BlockSpec(memory_space=pltpu.VMEM)
    return pl.pallas_call(
        kernel,
        name="diloco_step",
        out_shape=(
            jax.ShapeDtypeStruct((TOK, KV), bf16),
            jax.ShapeDtypeStruct((TOK, D), bf16),
            jax.ShapeDtypeStruct((1, COLS, KV), bf16),
            jax.ShapeDtypeStruct((1, COLS, KV), bf16),
            jax.ShapeDtypeStruct((1, SHARE, KV), f32),
            jax.ShapeDtypeStruct((1, SHARE, KV), f32),
        ),
        in_specs=[any_space] * 7,
        out_specs=(vmem,) * 6,
        scratch_shapes=[
            pltpu.VMEM((NF, TOK, COLS), bf16),
            pltpu.VMEM((NF, 1, COLS), f32),
            pltpu.VMEM((COLS, KV), bf16),
            pltpu.VMEM((COLS, KV), bf16),
            pltpu.VMEM((SHARE, KV), f32),
            pltpu.VMEM((SHARE, KV), f32),
            pltpu.VMEM((NF, TOK, KV), bf16),
            pltpu.VMEM((NF, TOK, COLS), bf16),
            pltpu.VMEM((NF, TOK, COLS), bf16),
            pltpu.VMEM((TOK, 128), f32),
            pltpu.VMEM((NF, TOK, COLS), bf16),
            pltpu.VMEM((NF, TOK, COLS), bf16),
            pltpu.VMEM((NF, TOK, KV), f32),
            pltpu.VMEM((TOK, KV), f32),
            pltpu.VMEM((TOK, KV), f32),
            pltpu.VMEM((TOK, KV), bf16),
            pltpu.VMEM((TOK, KV), bf16),
            pltpu.VMEM((K, NX - 1, XB, KC), bf16),
            pltpu.VMEM((K, NZ, NH, SHARE, KC), f32),
            pltpu.VMEM((K, NZ - 1, NH, SHARE, KC), f32),
            pltpu.VMEM((K, NH, SHARE, KC), f32),
            pltpu.VMEM((K, SHARE, KC), f32),
            pltpu.VMEM((NX, K, NZ, NH, SHARE, KC), bf16),
            pltpu.SemaphoreType.DMA((N_COPIES,)),
            pltpu.SemaphoreType.DMA((N_COPIES,)),
            pltpu.SemaphoreType.DMA((N_LOADS,)),
        ],
        compiler_params=pltpu.CompilerParams(
            collective_id=0, has_side_effects=True, vmem_limit_bytes=50 << 20
        ),
    )(
        tokens,
        norm_gain[None],
        key_weight,
        key_cotangent,
        fragment_local,
        fragment_global,
        outer_moment,
    )


def solution(mesh):
    return jax.shard_map(
        local,
        mesh=mesh,
        in_specs=(
            P(("replica", "fsdp"), None),
            P(),
            P("replica", "fsdp", None),
            P(("replica", "fsdp"), None),
            P("replica", "fsdp", None),
            P("fsdp", "replica", None),
            P("fsdp", "replica", None),
        ),
        out_specs=(
            P(("replica", "fsdp"), None),
            P(("replica", "fsdp"), None),
            P("replica", "fsdp", None),
            P("replica", "fsdp", None),
            P("fsdp", "replica", None),
            P("fsdp", "replica", None),
        ),
        check_vma=False,
    )
```

time: 1020 us -> 87.3 us (0.09)
  waiting for transfers between devices: 972 us -> 0 us
  Pallas kernels: 0 us -> 74.1 us
  other arithmetic: 16.8 us -> 0 us
  matrix products: 14.3 us -> 0 us
  between operations: 13.8 us -> 0.66 us
  local copies, waits for them, and re-layouts: 0.03 us -> 11.3 us
    psum x1 -> x0, waiting for transfers between devices: 709 us -> none  [local(): summed = lax.psum(local_rows, 'replica')]
    all_gather x2 -> x0, waiting for transfers between devices: 189 us -> none  [the longest x1 111 us: local(): lax.all_gather(global_new.astype(jnp.bfloat16), 'replica', axis=0, tiled=...]
    reduce_scatter x1 -> x0, waiting for transfers between devices: 74.4 us -> none  [local(): lax.psum_scatter((factor * lax.dot_general(columns, key_cotangent, (((0,)...]
    pallas_call x0 -> x1, Pallas kernels: none -> 74.1 us  [local(): pl.pallas_call(kernel, name='diloco_step', out_shape=(jax.ShapeDtypeStruc...]
    dot_general x3 -> x0, matrix products: 14.3 us -> none  [the longest x1 6.45 us: against_rows(): lax.dot_general(left, block_rows, (((1,), (1,)), ((), ())), preferred_ele...]
    unnamed x12 -> x18, local copies, waits for them, and re-layouts: 0.03 us -> 11.3 us
  transfers between devices with their start and end apart: 4 -> 0, of which waited for: 4 -> 0; matrix products, arithmetic and copies ran while one was open for 2% -> 0% of each run, Pallas kernels for 0% -> 0%
where the time goes in v1:
time: 87.3 us; the launch traced here: 86 us
  Pallas kernels  74.1 us (85%)
  local copies, waits for them, and re-layouts  11.3 us (13%)
    pallas_call x1, Pallas kernels, local(): pl.pallas_call(kernel, name='diloco_step', out_shape=(jax.ShapeDtypeStruc...  74.1 us
    unnamed x18, local copies, waits for them, and re-layouts  11.3 us

profile of v1, /device:TPU:8, one launch (start us, length us, event | category | flops | bytes accessed | tf_op | source)
XLA Modules:
  0.0 86.0 jit_solution(13384644361626899718)
XLA Ops:
  0.6 0.0 copy-start
  0.6 0.9 %copy-done = bf16[128,512]{1,0:T(8,128)(2,1)S(1)} copy-done((bf16[128,512]{1,0:T(8,128)(2,1)S(1)}, bf16[128,512]{1,0:T(8,128)(2,1)}, u32[]{:S(2)}) %copy-start) | copy-done | bytes 131096
  1.5 0.0 copy-start.1
  1.5 0.8 copy-done.1
  2.4 0.0 copy-start.2
  2.4 0.8 copy-done.2
  3.2 0.0 copy-start.3
  3.2 0.8 copy-done.3
  4.0 74.1 %diloco_step.1 = (bf16[128,512]{1,0:T(8,128)(2,1)S(1)}, bf16[128,8192]{1,0:T(8,128)(2,1)S(1)}, bf16[1,2048,512]{2,1,0:T(8,128)(2,1)}, bf16[1,2048,512]{2,1,0:T(8...) custom-call(bf16[128,8192]{1,0:T(8,128)(2,1)} %tokens.1, f32[1,8192]{1,0:T(1,128)S(1)} %bitcast.1, ...), custom_call_target="tpu_custom_call" | custom-call | tf_op jit(solution)/shard_map/diloco_step/pallas_call | solution.py:453
  78.0 0.7 copy.19
  78.7 0.0 copy-start.5
  78.7 1.3 %copy.20 = bf16[128,8192]{1,0:T(8,128)(2,1)} copy(bf16[128,8192]{1,0:T(8,128)(2,1)S(1)} %get-tuple-element.13) | data formatting | bytes 4194304
  80.0 1.0 %copy-done.5 = bf16[1,2048,512]{2,1,0:T(8,128)(2,1)S(1)} copy-done((bf16[1,2048,512]{2,1,0:T(8,128)(2,1)S(1)}, bf16[1,2048,512]{2,1,0:T(8,128)(2,1)}, u32[]{:S(2)}) %copy-start.5) | copy-done | bytes 2097176
  81.0 0.0 copy-start.4
  81.1 1.3 %copy.21 = bf16[1,2048,512]{2,1,0:T(8,128)(2,1)} copy(bf16[1,2048,512]{2,1,0:T(8,128)(2,1)S(1)} %copy-done.5) | data formatting | bytes 4194304
  82.4 1.0 %copy-done.4 = bf16[1,2048,512]{2,1,0:T(8,128)(2,1)S(1)} copy-done((bf16[1,2048,512]{2,1,0:T(8,128)(2,1)S(1)}, bf16[1,2048,512]{2,1,0:T(8,128)(2,1)}, u32[]{:S(2)}) %copy-start.4) | copy-done | bytes 2097176
  83.4 1.3 %copy.22 = bf16[1,2048,512]{2,1,0:T(8,128)(2,1)} copy(bf16[1,2048,512]{2,1,0:T(8,128)(2,1)S(1)} %copy-done.4) | data formatting | bytes 4194304
  84.7 0.6 copy.23
  85.3 0.6 copy.24
Async XLA Ops:
  0.6 0.9 %copy-start = (bf16[128,512]{1,0:T(8,128)(2,1)S(1)}, bf16[128,512]{1,0:T(8,128)(2,1)}, u32[]{:S(2)}) copy-start(bf16[128,512]{1,0:T(8,128)(2,1)} %cot_in.1) | copy-start | bytes 393220
  1.5 0.8 copy-start.1
  2.4 0.8 copy-start.2
  3.2 0.8 copy-start.3
  78.7 2.3 %copy-start.5 = (bf16[1,2048,512]{2,1,0:T(8,128)(2,1)S(1)}, bf16[1,2048,512]{2,1,0:T(8,128)(2,1)}, u32[]{:S(2)}) copy-start(bf16[1,2048,512]{2,1,0:T(8,128)(2,1)} %get-tuple-element.14) | copy-start | bytes 6291460
  81.0 2.3 %copy-start.4 = (bf16[1,2048,512]{2,1,0:T(8,128)(2,1)S(1)}, bf16[1,2048,512]{2,1,0:T(8,128)(2,1)}, u32[]{:S(2)}) copy-start(bf16[1,2048,512]{2,1,0:T(8,128)(2,1)} %get-tuple-element.15) | copy-start | bytes 6291460

commit v2 on v1

--- a/solution.py
+++ b/solution.py
@@ -24,9 +24,16 @@
 PR = TOK // PARTS
 SLAB = 512
 FACTOR = D ** (-0.5)
-N_COPIES = 128
+N_COPIES = 136
 N_LOADS = 16
 f32, bf16 = jnp.float32, jnp.bfloat16
+
+SCHEDULE = (
+    ("f0", "n1", "N2", "N3", "C0", "Q0", "X0", "f1", "B0", "X1", "n2", "f2", "X2", "n3", "Z0", "f3")
+    + ("Y0", "Z1", "X3", "b0", "U0", "Y1", "g0", "Z2", "U1", "V0", "b1", "Y2", "Z3", "g1")
+    + ("U2", "V1", "Y3", "b2", "g2", "K0", "U3", "V2", "L0", "b3", "g3", "V3", "W0")
+    + ("M0", "M1", "M2", "M3", "F0", "E0", "F1", "E1", "H0", "F2", "E2", "F3", "E3")
+)
 
 
 def kernel(
@@ -52,6 +59,8 @@
     cot,
     nin,
     nout,
+    n_relay_buf,
+    b_relay_buf,
     inv_s,
     bout,
     bin_,
@@ -62,6 +71,7 @@
     kc,
     xr,
     s1,
+    s1_sent,
     zr,
     s2,
     yr,
@@ -69,6 +79,8 @@
     send_sem,
     recv_sem,
     load_sem,
+    near_sem,
+    far_sem,
 ):
     r = lax.axis_index("replica")
     f = lax.axis_index("fsdp")
@@ -108,14 +120,67 @@
     load_outer = [load(global_in.at[0], glob), load(moment_in.at[0], moment)]
 
     barrier = pltpu.get_barrier_semaphore()
-    peers = (
-        [f_peer[q] for q in (1, 2, 3)]
-        + [x_peer(d) for d in range(1, NX)]
-        + [z_peer(d) for d in range(1, NZ)]
-        + [y_peer]
-    )
-    for peer in peers:
-        pl.semaphore_signal(barrier, 1, device_id=peer, device_id_type=MESH)
+
+    def tell(sem, device):
+        pl.semaphore_signal(sem, 1, device_id=device, device_id_type=MESH)
+
+    def fsdp_at(device, f):
+        return device[0], f
+
+    x_peers = [x_peer(d) for d in range(1, NX)]
+    far_peers = [z_peer(d) for d in range(1, NZ)] + [y_peer]
+    for peer in far_peers:
+        tell(barrier, fsdp_at(peer, 3))
+
+    @pl.when(core == 0)
+    def _():
+        tell(barrier, f_peer[2])
+        for peer in x_peers:
+            tell(barrier, peer)
+        tell(barrier, (r, 1))
+
+    @pl.when(f == 1)
+    def _():
+        for peer in x_peers:
+            tell(barrier, peer)
+
+    @pl.when(f == 3)
+    def _():
+        for peer in [(r, f)] + x_peers:
+            tell(barrier, fsdp_at(peer, 1))
+
+    def enter_near():
+        @pl.when(core == 0)
+        def _():
+            pl.semaphore_wait(barrier, NX)
+
+        @pl.when(f == 1)
+        def _():
+            pl.semaphore_wait(barrier, 2 * NX + 1)
+            tell(near_sem, (r, 0))
+            tell(near_sem, (r, 3))
+
+        @pl.when(f == 3)
+        def _():
+            pl.semaphore_wait(near_sem, 1)
+            tell(near_sem, (r, 2))
+
+    def enter_chip():
+        @pl.when(core == 0)
+        def _():
+            pl.semaphore_wait(near_sem, 1)
+
+    def hear_far():
+        @pl.when(f == 3)
+        def _():
+            pl.semaphore_wait(barrier, NF * len(far_peers))
+            for other in range(3):
+                tell(far_sem, (r, other))
+
+    def enter_far():
+        @pl.when(f != 3)
+        def _():
+            pl.semaphore_wait(far_sem, 1)
 
     copies = []
 
@@ -161,8 +226,16 @@
 
         lax.fori_loop(1, NF, others, 0)
 
-    def send_normed(c, q):
-        return remote(nout.at[q, rows_of(c)], nin.at[q, rows_of(c)], f_peer[q])
+    def send_block(out, into, relay, c, q):
+        rows = rows_of(c)
+        if q == 3:
+            return remote(out.at[3, rows], relay.at[rows], f_peer[1])
+        return remote(out.at[q, rows], into.at[q, rows], f_peer[q])
+
+    def pass_on(into, relay, c, copy):
+        rows = rows_of(c)
+        copy.wait_recv()
+        return remote(relay.at[rows], into.at[3, rows], f_peer[2])
 
     def back_products():
         left = cot[...].reshape(NF * TOK, KV)
@@ -179,9 +252,6 @@
             return 0
 
         lax.fori_loop(0, COLS // 256, tile, 0)
-
-    def send_back(c, q):
-        return remote(bout.at[q, rows_of(c)], bin_.at[q, rows_of(c)], f_peer[q])
 
     def key_products():
         left = nin[...].reshape(NF * TOK, COLS)
@@ -257,19 +327,20 @@
                 for d in range(NX - 1):
                     total = total + xr[k, d, rows, :].astype(f32)
                 s1[k, zi, h] = total
+                s1_sent[k, zi, h] = total.astype(bf16)
                 return 0
 
             lax.fori_loop(0, NZ, one, 0)
 
     def z_scatter(k):
         return [
-            remote(s1.at[k, (z + d) % NZ], zr.at[k, d - 1], z_peer(d)) for d in range(1, NZ)
+            remote(s1_sent.at[k, (z + d) % NZ], zr.at[k, d - 1], z_peer(d)) for d in range(1, NZ)
         ]
 
     def z_sum(k):
         total = s1[k, z]
         for d in range(NZ - 1):
-            total = total + zr[k, d]
+            total = total + zr[k, d].astype(f32)
         s2[k] = total
 
     def y_scatter(k):
@@ -316,152 +387,166 @@
         for copy in group if isinstance(group, list) else [group]:
             copy.wait_recv()
 
+    live = {}
+
+    def normed(c):
+        normalise(c)
+        live["nr", c] = send_block(nout, nin, n_relay_buf, c, 3)
+        live["nl", c] = send_block(nout, nin, n_relay_buf, c, 1)
+
+    def y_normed(c):
+        live["nc", c] = send_block(nout, nin, n_relay_buf, c, 2)
+
+    def pass_normed(c):
+        live["np", c] = pass_on(nin, n_relay_buf, c, live["nr", c])
+
+    def cot_on(_):
+        arrive(live["cot2", 0])
+        live["cot3", 0] = remote(cot.at[2], cot.at[3], f_peer[1])
+
+    def back(_):
+        load_cot.wait()
+        load_weight.wait()
+        arrive([live["cot1", 0], live["cot3", 0]])
+        back_products()
+        for c in range(PARTS):
+            live["br", c] = send_block(bout, bin_, b_relay_buf, c, 3)
+            live["bl", c] = send_block(bout, bin_, b_relay_buf, c, 1)
+
+    def y_back(c):
+        live["bc", c] = send_block(bout, bin_, b_relay_buf, c, 2)
+
+    def pass_back(c):
+        live["bp", c] = pass_on(bin_, b_relay_buf, c, live["br", c])
+
+    def on_x(k):
+        arrive(live["x", k])
+        if k == 0:
+            load_frag.wait()
+        x_sum(k)
+        if k == 0:
+            enter_far()
+        live["z", k] = z_scatter(k)
+
+    def on_z(k):
+        arrive(live["z", k])
+        z_sum(k)
+        live["y", k] = y_scatter(k)
+
+    def on_y(k):
+        if k == 0:
+            for copy in load_outer:
+                copy.wait()
+        arrive(live["y", k])
+        update(k)
+        live["yg", k] = y_gather(k)
+
+    def on_yg(k):
+        arrive(live["yg", k])
+        live["zg", k] = z_gather(k)
+
+    def on_zg(k):
+        arrive(live["zg", k])
+        live["xg", k] = x_gather(k)
+
+    def on_xg(k):
+        arrive(live["xg", k])
+        for e in range(1, NX):
+            mix(k, e)
+
+    def keys(_):
+        arrive([live[n, c] for n in ("nl", "nc", "np") for c in range(PARTS)])
+        key_products()
+        live["k3", 0] = remote(kp.at[3], kx, f_peer[1])
+        live["k1", 0] = remote(kp.at[1], kp1, f_peer[1])
+
+    def keys_on(_):
+        arrive(live["k3", 0])
+        ksend[...] = (FACTOR * (kp[2] + kx[...])).astype(bf16)
+        live["k2", 0] = remote(ksend, kc, f_peer[2])
+
+    def keys_out(_):
+        arrive([live["k1", 0], live["k2", 0]])
+        key_out[...] = (FACTOR * (kp[0] + kp1[...]) + kc[...].astype(f32)).astype(bf16)
+
+    def tokens_out(c):
+        arrive([live[n, c] for n in ("bl", "bc", "bp")])
+        finish_tokens(c)
+
+    steps = {
+        "N": normed,
+        "n": y_normed,
+        "f": pass_normed,
+        "C": cot_on,
+        "Q": lambda _: hear_far(),
+        "B": back,
+        "b": y_back,
+        "g": pass_back,
+        "X": on_x,
+        "Z": on_z,
+        "Y": on_y,
+        "U": on_yg,
+        "V": on_zg,
+        "E": on_xg,
+        "K": keys,
+        "L": keys_on,
+        "H": keys_out,
+        "W": lambda _: weight_products(),
+        "M": lambda k: mix(k, 0),
+        "F": tokens_out,
+    }
+
     for copy in load_tok + load_gain:
         copy.wait()
     normalise(0)
-    pl.semaphore_wait(barrier, len(peers))
-    cot1 = remote(cot_in, cot.at[1], f_peer[1])
-    cot2 = remote(cot_in, cot.at[2], f_peer[2])
-    xs = [x_scatter(0), x_scatter(1)]
-    nq = {}
-    bq = {}
-    for q in (2, 3, 1):
-        nq[0, q] = send_normed(0, q)
-    xs += [x_scatter(2), x_scatter(3)]
-    for c in range(1, PARTS):
-        normalise(c)
-        nq[c, 1] = send_normed(c, 1)
-    arrive(cot2)
-    cot3 = remote(cot.at[2], cot.at[3], f_peer[1])
-    nq[1, 2] = send_normed(1, 2)
-
-    load_frag.wait()
-    arrive(xs[0])
-    x_sum(0)
-    zs = [z_scatter(0)]
-    nq[1, 3] = send_normed(1, 3)
-    nq[2, 2] = send_normed(2, 2)
-    load_cot.wait()
-    load_weight.wait()
-    arrive(cot1)
-    arrive(cot3)
-    back_products()
-    for c in range(PARTS):
-        bq[c, 1] = send_back(c, 1)
-
-    arrive(xs[1])
-    x_sum(1)
-    zs.append(z_scatter(1))
-    arrive(zs[0])
-    z_sum(0)
-    ys = [y_scatter(0)]
-    nq[2, 3] = send_normed(2, 3)
-    nq[3, 2] = send_normed(3, 2)
-    for copy in load_outer:
-        copy.wait()
-
-    arrive(xs[2])
-    x_sum(2)
-    zs.append(z_scatter(2))
-    arrive(zs[1])
-    z_sum(1)
-    ys.append(y_scatter(1))
-    arrive(ys[0])
-    update(0)
-    yg = [y_gather(0)]
-    nq[3, 3] = send_normed(3, 3)
-    bq[0, 2] = send_back(0, 2)
-
-    arrive(xs[3])
-    x_sum(3)
-    zs.append(z_scatter(3))
-    arrive(zs[2])
-    z_sum(2)
-    ys.append(y_scatter(2))
-    arrive(ys[1])
-    update(1)
-    yg.append(y_gather(1))
-    arrive(yg[0])
-    zg = [z_gather(0)]
-    bq[0, 3] = send_back(0, 3)
-    bq[1, 2] = send_back(1, 2)
-
-    arrive(zs[3])
-    z_sum(3)
-    ys.append(y_scatter(3))
-    arrive(ys[2])
-    update(2)
-    yg.append(y_gather(2))
-    arrive(yg[1])
-    zg.append(z_gather(1))
-    arrive(zg[0])
-    xg = [x_gather(0)]
-    bq[1, 3] = send_back(1, 3)
-    bq[2, 2] = send_back(2, 2)
-    for c in range(PARTS):
-        for q in (1, 2, 3):
-            arrive(nq[c, q])
-    key_products()
-    k3 = remote(kp.at[3], kx, f_peer[1])
-    k1 = remote(kp.at[1], kp1, f_peer[1])
-
-    arrive(ys[3])
-    update(3)
-    yg.append(y_gather(3))
-    arrive(yg[2])
-    zg.append(z_gather(2))
-    arrive(zg[1])
-    xg.append(x_gather(1))
-    arrive(k3)
-    ksend[...] = (FACTOR * (kp[2] + kx[...])).astype(bf16)
-    k2 = remote(ksend, kc, f_peer[2])
-    bq[2, 3] = send_back(2, 3)
-    arrive(yg[3])
-    zg.append(z_gather(3))
-    bq[3, 2] = send_back(3, 2)
-    bq[3, 3] = send_back(3, 3)
-    arrive(zg[2])
-    xg.append(x_gather(2))
-    arrive(zg[3])
-    xg.append(x_gather(3))
-    weight_products()
-
-    for k in range(K):
-        mix(k, 0)
-    for k in range(K):
-        for c in range(PARTS):
-            if c == k:
-                for q in (1, 2, 3):
-                    arrive(bq[c, q])
-                finish_tokens(c)
-        arrive(xg[k])
-        for e in range(1, NX):
-            mix(k, e)
-        if k == 1:
-            arrive(k1)
-            arrive(k2)
-            key_out[...] = (FACTOR * (kp[0] + kp1[...]) + kc[...].astype(f32)).astype(bf16)
+    enter_near()
+    live["cot2", 0] = remote(cot_in, cot.at[2], f_peer[2])
+    live["x", 0] = x_scatter(0)
+    y_normed(0)
+    for k in range(1, K):
+        live["x", k] = x_scatter(k)
+    normalise(1)
+    enter_chip()
+    for c in range(2):
+        live["nr", c] = send_block(nout, nin, n_relay_buf, c, 3)
+        live["nl", c] = send_block(nout, nin, n_relay_buf, c, 1)
+    live["cot1", 0] = remote(cot_in, cot.at[1], f_peer[1])
+    for step in SCHEDULE:
+        steps[step[0]](int(step[1:]))
     for copy in copies:
         copy.wait_send()
+
+
+def write_out(*refs):
+    sources, targets, sem = refs[:6], refs[6:12], refs[12]
+    copies = [
+        pltpu.make_async_copy(s, t, sem.at[i])
+        for i, (s, t) in enumerate(zip(sources, targets, strict=True))
+    ]
+    for copy in copies:
+        copy.start()
+    for copy in copies:
+        copy.wait()
 
 
 def local(
     tokens, norm_gain, key_weight, key_cotangent, fragment_local, fragment_global, outer_moment
 ):
-    any_space = pl.BlockSpec(memory_space=pl.ANY)
+    hbm = pl.BlockSpec(memory_space=pltpu.HBM)
     vmem = pl.BlockSpec(memory_space=pltpu.VMEM)
-    return pl.pallas_call(
+    shapes = (
+        jax.ShapeDtypeStruct((TOK, KV), bf16),
+        jax.ShapeDtypeStruct((TOK, D), bf16),
+        jax.ShapeDtypeStruct((1, COLS, KV), bf16),
+        jax.ShapeDtypeStruct((1, COLS, KV), bf16),
+        jax.ShapeDtypeStruct((1, SHARE, KV), f32),
+        jax.ShapeDtypeStruct((1, SHARE, KV), f32),
+    )
+    results = pl.pallas_call(
         kernel,
         name="diloco_step",
-        out_shape=(
-            jax.ShapeDtypeStruct((TOK, KV), bf16),
-            jax.ShapeDtypeStruct((TOK, D), bf16),
-            jax.ShapeDtypeStruct((1, COLS, KV), bf16),
-            jax.ShapeDtypeStruct((1, COLS, KV), bf16),
-            jax.ShapeDtypeStruct((1, SHARE, KV), f32),
-            jax.ShapeDtypeStruct((1, SHARE, KV), f32),
-        ),
-        in_specs=[any_space] * 7,
+        out_shape=shapes,
+        in_specs=[hbm] * 7,
         out_specs=(vmem,) * 6,
         scratch_shapes=[
             pltpu.VMEM((NF, TOK, COLS), bf16),
@@ -473,6 +558,8 @@
             pltpu.VMEM((NF, TOK, KV), bf16),
             pltpu.VMEM((NF, TOK, COLS), bf16),
             pltpu.VMEM((NF, TOK, COLS), bf16),
+            pltpu.VMEM((TOK, COLS), bf16),
+            pltpu.VMEM((TOK, COLS), bf16),
             pltpu.VMEM((TOK, 128), f32),
             pltpu.VMEM((NF, TOK, COLS), bf16),
             pltpu.VMEM((NF, TOK, COLS), bf16),
@@ -483,26 +570,43 @@
             pltpu.VMEM((TOK, KV), bf16),
             pltpu.VMEM((K, NX - 1, XB, KC), bf16),
             pltpu.VMEM((K, NZ, NH, SHARE, KC), f32),
-            pltpu.VMEM((K, NZ - 1, NH, SHARE, KC), f32),
+            pltpu.VMEM((K, NZ, NH, SHARE, KC), bf16),
+            pltpu.VMEM((K, NZ - 1, NH, SHARE, KC), bf16),
             pltpu.VMEM((K, NH, SHARE, KC), f32),
             pltpu.VMEM((K, SHARE, KC), f32),
             pltpu.VMEM((NX, K, NZ, NH, SHARE, KC), bf16),
             pltpu.SemaphoreType.DMA((N_COPIES,)),
             pltpu.SemaphoreType.DMA((N_COPIES,)),
             pltpu.SemaphoreType.DMA((N_LOADS,)),
+            pltpu.SemaphoreType.REGULAR,
+            pltpu.SemaphoreType.REGULAR,
         ],
         compiler_params=pltpu.CompilerParams(
-            collective_id=0, has_side_effects=True, vmem_limit_bytes=50 << 20
+            collective_id=0, has_side_effects=True, vmem_limit_bytes=36 << 20
         ),
     )(
-        tokens,
-        norm_gain[None],
-        key_weight,
-        key_cotangent,
-        fragment_local,
-        fragment_global,
-        outer_moment,
+        *(
+            pltpu.with_memory_space_constraint(a, pltpu.HBM)
+            for a in (
+                tokens,
+                norm_gain[None],
+                key_weight,
+                key_cotangent,
+                fragment_local,
+                fragment_global,
+                outer_moment,
+            )
+        )
     )
+    return pl.pallas_call(
+        write_out,
+        name="write_out",
+        out_shape=shapes,
+        in_specs=[vmem] * 6,
+        out_specs=(hbm,) * 6,
+        scratch_shapes=[pltpu.SemaphoreType.DMA((6,))],
+        compiler_params=pltpu.CompilerParams(vmem_limit_bytes=1 << 20),
+    )(*results)
 
 
 def solution(mesh):

time: 87.3 us -> 75.2 us (0.86); the launches traced: 86 us -> 75.1 us
  local copies, waits for them, and re-layouts: 11.3 us -> 0 us
    unnamed x18 -> x0, local copies, waits for them, and re-layouts: 11.3 us -> none
    pallas_call x1 -> x2, Pallas kernels: 74.1 us -> 74.5 us  [the longest x1 71.7 us: local(): pl.pallas_call(kernel, name='diloco_step', out_shape=shapes, in_specs=[hb...]
where the time goes in v2:
time: 75.2 us; the launch traced here: 75.1 us
  Pallas kernels  74.5 us (99%)
    pallas_call x1, Pallas kernels, local(): pl.pallas_call(kernel, name='diloco_step', out_shape=shapes, in_specs=[hb...  71.7 us
    pallas_call x1, Pallas kernels, local(): pl.pallas_call(write_out, name='write_out', out_shape=shapes, in_specs=[v...  2.8 us

profile of v2, /device:TPU:8, one launch (start us, length us, event | category | flops | bytes accessed | tf_op | source)
XLA Modules:
  0.0 75.1 jit_solution(15092344411379636149)
XLA Ops:
  0.6 71.7 %diloco_step.1 = (bf16[128,512]{1,0:T(8,128)(2,1)S(1)}, bf16[128,8192]{1,0:T(8,128)(2,1)S(1)}, bf16[1,2048,512]{2,1,0:T(8,128)(2,1)S(1)}, bf16[1,2048,512]{2,1,0...) custom-call(bf16[128,8192]{1,0:T(8,128)(2,1)} %tokens.1, f32[1,8192]{1,0:T(1,128)} %bitcast.1, ...), custom_call_target="tpu_custom_call" | custom-call | tf_op jit(solution)/shard_map/diloco_step/pallas_call | solution.py:545
  72.3 2.8 %write_out.1 = (bf16[128,512]{1,0:T(8,128)(2,1)}, bf16[128,8192]{1,0:T(8,128)(2,1)}, bf16[1,2048,512]{2,1,0:T(8,128)(2,1)}, bf16[1,2048,512]{2,1,0:T(8,128)(2,1)...) custom-call(bf16[128,512]{1,0:T(8,128)(2,1)S(1)} %get-tuple-element.12.refs_0_, ...), custom_call_target="tpu_custom_call" | custom-call | tf_op jit(solution)/shard_map/write_out/pallas_call | solution.py:601

commit v3 on v2

--- a/solution.py
+++ b/solution.py
@@ -29,9 +29,9 @@
 f32, bf16 = jnp.float32, jnp.bfloat16
 
 SCHEDULE = (
-    ("f0", "n1", "N2", "N3", "C0", "Q0", "X0", "f1", "B0", "X1", "n2", "f2", "X2", "n3", "Z0", "f3")
-    + ("Y0", "Z1", "X3", "b0", "U0", "Y1", "g0", "Z2", "U1", "V0", "b1", "Y2", "Z3", "g1")
-    + ("U2", "V1", "Y3", "b2", "g2", "K0", "U3", "V2", "L0", "b3", "g3", "V3", "W0")
+    ("f0", "n1", "N2", "N3", "C0", "Q0", "X0", "f1", "n2", "B0", "X1", "f2", "n3", "Z0", "f3", "X2")
+    + ("Z1", "b0", "Y0", "X3", "g0", "Z2", "Y1", "b1", "V0", "Z3", "g1", "Y2")
+    + ("b2", "V1", "Y3", "g2", "b3", "V2", "K0", "g3", "L0", "V3", "W0")
     + ("M0", "M1", "M2", "M3", "F0", "E0", "F1", "E1", "H0", "F2", "E2", "F3", "E3")
 )
 
@@ -75,6 +75,7 @@
     zr,
     s2,
     yr,
+    base,
     gx,
     send_sem,
     recv_sem,
@@ -317,10 +318,10 @@
     def x_sum(k):
         lanes = pl.ds(k * KC, KC)
         for h in range(NH):
-            base = ((yh + h) % NH) * (NZ * SHARE)
+            first = ((yh + h) % NH) * (NZ * SHARE)
 
             def one(zi, _):
-                at = base + zi * SHARE
+                at = first + zi * SHARE
                 own = pl.ds(pl.multiple_of(x * XB + at, SHARE), SHARE)
                 rows = pl.ds(pl.multiple_of(at, SHARE), SHARE)
                 total = frag[own, lanes].astype(f32)
@@ -341,24 +342,29 @@
         total = s1[k, z]
         for d in range(NZ - 1):
             total = total + zr[k, d].astype(f32)
-        s2[k] = total
-
-    def y_scatter(k):
-        return remote(s2.at[k, 1], yr.at[k], y_peer)
+        s2[k] = total.astype(bf16)
+
+    pull = outer_rate * (1.0 + momentum_decay)
+
+    def outer_base():
+        g = glob[...]
+        base[0] = g - (pull * g + (outer_rate * momentum_decay**2) * moment[...])
+        return remote(base.at[0], base.at[1], y_peer)
+
+    def y_swap(k):
+        return remote(s2.at[k], yr.at[k], y_peer)
 
     def update(k):
         lanes = pl.ds(k * KC, KC)
-        mean = (s2[k, 0] + yr[k]) * (1.0 / REPLICAS)
-        g = glob[:, lanes]
-        outer_grad = g - mean
-        m = momentum_decay * moment[:, lanes] + outer_grad
-        g = g - outer_rate * (outer_grad + momentum_decay * m)
-        moment_new[0, :, lanes] = m
-        global_new[0, :, lanes] = g
-        gx[0, k, 0, 0] = g.astype(bf16)
-
-    def y_gather(k):
-        return remote(gx.at[0, k, 0, 0], gx.at[0, k, 0, 1], y_peer)
+        for h in range(NH):
+            mean = (s2[k, h].astype(f32) + yr[k, 1 - h].astype(f32)) * (1.0 / REPLICAS)
+            gx[0, k, 0, h] = (base[h, :, lanes] + pull * mean).astype(bf16)
+            if h == 0:
+                g = glob[:, lanes]
+                outer_grad = g - mean
+                m = momentum_decay * moment[:, lanes] + outer_grad
+                moment_new[0, :, lanes] = m
+                global_new[0, :, lanes] = g - outer_rate * (outer_grad + momentum_decay * m)
 
     def z_gather(k):
         return [remote(gx.at[0, k, 0], gx.at[0, k, d], z_peer(d)) for d in range(1, NZ)]
@@ -370,10 +376,10 @@
         lanes = pl.ds(k * KC, KC)
         xi = (x + NX - e) % NX
         for h in range(NH):
-            base = xi * XB + ((yh + h) % NH) * (NZ * SHARE)
+            first = xi * XB + ((yh + h) % NH) * (NZ * SHARE)
 
             def one(d, _):
-                at = base + ((z + NZ - d) % NZ) * SHARE
+                at = first + ((z + NZ - d) % NZ) * SHARE
                 rows = pl.ds(pl.multiple_of(at, SHARE), SHARE)
                 mixed[0, rows, lanes] = (
                     mix_keep * frag[rows, lanes].astype(f32)
@@ -426,23 +432,21 @@
         x_sum(k)
         if k == 0:
             enter_far()
+            for copy in load_outer:
+                copy.wait()
+            live["base", 0] = outer_base()
         live["z", k] = z_scatter(k)
 
     def on_z(k):
         arrive(live["z", k])
         z_sum(k)
-        live["y", k] = y_scatter(k)
+        live["y", k] = y_swap(k)
 
     def on_y(k):
         if k == 0:
-            for copy in load_outer:
-                copy.wait()
+            arrive(live["base", 0])
         arrive(live["y", k])
         update(k)
-        live["yg", k] = y_gather(k)
-
-    def on_yg(k):
-        arrive(live["yg", k])
         live["zg", k] = z_gather(k)
 
     def on_zg(k):
@@ -485,7 +489,6 @@
         "X": on_x,
         "Z": on_z,
         "Y": on_y,
-        "U": on_yg,
         "V": on_zg,
         "E": on_xg,
         "K": keys,
@@ -496,15 +499,14 @@
         "F": tokens_out,
     }
 
+    enter_near()
+    live["cot2", 0] = remote(cot_in, cot.at[2], f_peer[2])
+    for k in range(K):
+        live["x", k] = x_scatter(k)
     for copy in load_tok + load_gain:
         copy.wait()
     normalise(0)
-    enter_near()
-    live["cot2", 0] = remote(cot_in, cot.at[2], f_peer[2])
-    live["x", 0] = x_scatter(0)
     y_normed(0)
-    for k in range(1, K):
-        live["x", k] = x_scatter(k)
     normalise(1)
     enter_chip()
     for c in range(2):
@@ -572,8 +574,9 @@
             pltpu.VMEM((K, NZ, NH, SHARE, KC), f32),
             pltpu.VMEM((K, NZ, NH, SHARE, KC), bf16),
             pltpu.VMEM((K, NZ - 1, NH, SHARE, KC), bf16),
-            pltpu.VMEM((K, NH, SHARE, KC), f32),
-            pltpu.VMEM((K, SHARE, KC), f32),
+            pltpu.VMEM((K, NH, SHARE, KC), bf16),
+            pltpu.VMEM((K, NH, SHARE, KC), bf16),
+            pltpu.VMEM((NH, SHARE, KV), f32),
             pltpu.VMEM((NX, K, NZ, NH, SHARE, KC), bf16),
             pltpu.SemaphoreType.DMA((N_COPIES,)),
             pltpu.SemaphoreType.DMA((N_COPIES,)),

time: 75.2 us -> 73.5 us (0.977)
  Pallas kernels: 74.5 us -> 72.8 us
    pallas_call x1, Pallas kernels: 71.7 us -> 70 us  [local(): pl.pallas_call(kernel, name='diloco_step', out_shape=shapes, in_specs=[hb...]
where the time goes in v3:
time: 73.5 us; the launch traced here: 73.4 us
  Pallas kernels  72.8 us (99%)
    pallas_call x1, Pallas kernels, local(): pl.pallas_call(kernel, name='diloco_step', out_shape=shapes, in_specs=[hb...  70 us
    pallas_call x1, Pallas kernels, local(): pl.pallas_call(write_out, name='write_out', out_shape=shapes, in_specs=[v...  2.8 us

profile of v3, /device:TPU:8, one launch (start us, length us, event | category | flops | bytes accessed | tf_op | source)
XLA Modules:
  0.0 73.4 jit_solution(15558575391989676643)
XLA Ops:
  0.6 70.0 %diloco_step.1 = (bf16[128,512]{1,0:T(8,128)(2,1)S(1)}, bf16[128,8192]{1,0:T(8,128)(2,1)S(1)}, bf16[1,2048,512]{2,1,0:T(8,128)(2,1)S(1)}, bf16[1,2048,512]{2,1,0...) custom-call(bf16[128,8192]{1,0:T(8,128)(2,1)} %tokens.1, f32[1,8192]{1,0:T(1,128)} %bitcast.1, ...), custom_call_target="tpu_custom_call" | custom-call | tf_op jit(solution)/shard_map/diloco_step/pallas_call | solution.py:547
  70.6 2.8 %write_out.1 = (bf16[128,512]{1,0:T(8,128)(2,1)}, bf16[128,8192]{1,0:T(8,128)(2,1)}, bf16[1,2048,512]{2,1,0:T(8,128)(2,1)}, bf16[1,2048,512]{2,1,0:T(8,128)(2,1)...) custom-call(bf16[128,512]{1,0:T(8,128)(2,1)S(1)} %get-tuple-element.12.refs_0_, ...), custom_call_target="tpu_custom_call" | custom-call | tf_op jit(solution)/shard_map/write_out/pallas_call | solution.py:604

commit v4 on v3

--- a/solution.py
+++ b/solution.py
@@ -31,7 +31,7 @@
 SCHEDULE = (
     ("f0", "n1", "N2", "N3", "C0", "Q0", "X0", "f1", "n2", "B0", "X1", "f2", "n3", "Z0", "f3", "X2")
     + ("Z1", "b0", "Y0", "X3", "g0", "Z2", "Y1", "b1", "V0", "Z3", "g1", "Y2")
-    + ("b2", "V1", "Y3", "g2", "b3", "V2", "K0", "g3", "L0", "V3", "W0")
+    + ("b2", "V1", "Y3", "g2", "b3", "V2", "K0", "g3", "V3", "L0", "W0")
     + ("M0", "M1", "M2", "M3", "F0", "E0", "F1", "E1", "H0", "F2", "E2", "F3", "E3")
 )
 

time: 73.5 us -> 73.5 us (level)
  no operation moved by 1% of the time
where the time goes in v4:
time: 73.5 us; the launch traced here: 73.4 us
  Pallas kernels  72.8 us (99%)
    pallas_call x1, Pallas kernels, local(): pl.pallas_call(kernel, name='diloco_step', out_shape=shapes, in_specs=[hb...  70 us
    pallas_call x1, Pallas kernels, local(): pl.pallas_call(write_out, name='write_out', out_shape=shapes, in_specs=[v...  2.8 us

profile of v4, /device:TPU:8, one launch (start us, length us, event | category | flops | bytes accessed | tf_op | source)
XLA Modules:
  0.0 73.4 jit_solution(4042878714789327067)
XLA Ops:
  0.6 70.0 %diloco_step.1 = (bf16[128,512]{1,0:T(8,128)(2,1)S(1)}, bf16[128,8192]{1,0:T(8,128)(2,1)S(1)}, bf16[1,2048,512]{2,1,0:T(8,128)(2,1)S(1)}, bf16[1,2048,512]{2,1,0...) custom-call(bf16[128,8192]{1,0:T(8,128)(2,1)} %tokens.1, f32[1,8192]{1,0:T(1,128)} %bitcast.1, ...), custom_call_target="tpu_custom_call" | custom-call | tf_op jit(solution)/shard_map/diloco_step/pallas_call | solution.py:547
  70.6 2.8 %write_out.1 = (bf16[128,512]{1,0:T(8,128)(2,1)}, bf16[128,8192]{1,0:T(8,128)(2,1)}, bf16[1,2048,512]{2,1,0:T(8,128)(2,1)}, bf16[1,2048,512]{2,1,0:T(8,128)(2,1)...) custom-call(bf16[128,512]{1,0:T(8,128)(2,1)S(1)} %get-tuple-element.12.refs_0_, ...), custom_call_target="tpu_custom_call" | custom-call | tf_op jit(solution)/shard_map/write_out/pallas_call | solution.py:604
